TPU v7x, 128 devices: a whole 4x4x4 slice. The times are simulated.
128 devices in a mesh: dp: 8 (over z, core), ctx: 16 (over y, x).
Axes of the slice: x: 4, y: 4, z: 4, core: 2. Of those that a mesh axis runs over, the one named last changes fastest.
Arguments:
- attn_in: bfloat16 [8, 2048, 4096], P('dp', 'ctx'), may hold values from -6 to 6
- attn_mix: bfloat16 [8, 2048, 4096], P('dp', 'ctx'), may hold values from -6 to 6
- mlp_in: bfloat16 [8, 2048, 4096], P('dp', 'ctx'), may hold values from -6 to 6
- mlp_act: bfloat16 [8, 2048, 14336], P('dp', 'ctx'), may hold values from -6 to 6
- grad_query: bfloat16 [8, 2048, 4096], P('dp', 'ctx'), may hold values from -0.19921875 to 0.19921875
- grad_key: bfloat16 [8, 2048, 1024], P('dp', 'ctx'), may hold values from -0.19921875 to 0.19921875
- grad_value: bfloat16 [8, 2048, 1024], P('dp', 'ctx'), may hold values from -0.19921875 to 0.19921875
- grad_output: bfloat16 [8, 2048, 4096], P('dp', 'ctx'), may hold values from -0.19921875 to 0.19921875
- grad_gate: bfloat16 [8, 2048, 14336], P('dp', 'ctx'), may hold values from -0.19921875 to 0.19921875
- grad_up: bfloat16 [8, 2048, 14336], P('dp', 'ctx'), may hold values from -0.19921875 to 0.19921875
- grad_down: bfloat16 [8, 2048, 4096], P('dp', 'ctx'), may hold values from -0.19921875 to 0.19921875
- proj_attn: bfloat16 [4096, 64], replicated, may hold values from -0.09375 to 0.09375
- proj_mix: bfloat16 [4096, 64], replicated, may hold values from -0.09375 to 0.09375
- proj_mlp: bfloat16 [4096, 64], replicated, may hold values from -0.09375 to 0.09375
- proj_act: bfloat16 [14336, 64], replicated, may hold values from -0.046875 to 0.046875
- proj_query: bfloat16 [4096, 64], replicated, may hold values from -0.09375 to 0.09375
- proj_key: bfloat16 [1024, 64], replicated, may hold values from -0.1875 to 0.1875
- proj_value: bfloat16 [1024, 64], replicated, may hold values from -0.1875 to 0.1875
- proj_output: bfloat16 [4096, 64], replicated, may hold values from -0.09375 to 0.09375
- proj_gate: bfloat16 [14336, 64], replicated, may hold values from -0.046875 to 0.046875
- proj_upward: bfloat16 [14336, 64], replicated, may hold values from -0.046875 to 0.046875
- proj_down: bfloat16 [4096, 64], replicated, may hold values from -0.09375 to 0.09375
- seq_counts: int32 [8], P('dp'), may hold values from 128 to 2048, as said below
- example_ids: int32 [8], replicated, may hold values from 0 to 7, each once
Outputs:
- store: float32 [8, 7, 4096], P('dp', None, 'ctx')
Inputs may be any that keep to these rules, and one draw needn't show every extreme that they name: `seq_counts`: every count is a multiple of 128; some sequence has all 2048 tokens. `example_ids`: a permutation: every store row receives exactly one sequence.
All inputs are finite; a program needn't handle non-finite values.
Results may differ from a plain program's by a relative error of at most 0.004.
Values sent between devices are 32-bit elements; how exact they have to be, the bound alone decides.
No kernel may reach another device: no remote copies, remote signals or barrier semaphores. Data moves between devices by JAX's collectives and lax.ppermute only.
A program may use at most 128 MiB of HBM per device.

v0:
```python
import jax
import jax.numpy as jnp
from jax import lax
from jax.sharding import PartitionSpec as P


def project_rows(acts, projection):
    return jnp.dot(acts[0], projection, preferred_element_type=jnp.float32).astype(jnp.bfloat16)


def outer_sum(grads_proj, inputs_proj):
    product = lax.dot_general(
        grads_proj, inputs_proj, (((0,), (0,)), ((), ())), preferred_element_type=jnp.float32
    )
    return product.reshape(-1)


def reduce_positions(values):
    summed = lax.psum(values, "ctx")
    width = values.shape[2] // lax.axis_size("ctx")
    return lax.dynamic_slice_in_dim(summed, lax.axis_index("ctx") * width, width, 2)


def pick_owned(gathered, example_ids):
    owner = lax.axis_index("dp")
    weights = (example_ids == owner).astype(jnp.float32)
    return jnp.sum(weights[:, None, None] * gathered, axis=0, keepdims=True)


def shards(
    attn_in,
    attn_mix,
    mlp_in,
    mlp_act,
    grad_query,
    grad_key,
    grad_value,
    grad_output,
    grad_gate,
    grad_up,
    grad_down,
    proj_attn,
    proj_mix,
    proj_mlp,
    proj_act,
    proj_query,
    proj_key,
    proj_value,
    proj_output,
    proj_gate,
    proj_upward,
    proj_down,
    seq_counts,
    example_ids,
):
    length_dev = attn_in.shape[1]
    first_pos = lax.axis_index("ctx") * length_dev
    limit_pos = seq_counts[0]
    live_rows = (first_pos + jnp.arange(length_dev, dtype=jnp.int32) < limit_pos).astype(
        jnp.bfloat16
    )[:, None]
    attn_p = project_rows(attn_in, proj_attn)
    mix_p = project_rows(attn_mix, proj_mix)
    mlp_p = project_rows(mlp_in, proj_mlp)
    act_p = project_rows(mlp_act, proj_act)
    pairs = [
        (grad_query, proj_query, attn_p),
        (grad_key, proj_key, attn_p),
        (grad_value, proj_value, attn_p),
        (grad_output, proj_output, mix_p),
        (grad_gate, proj_gate, mlp_p),
        (grad_up, proj_upward, mlp_p),
        (grad_down, proj_down, act_p),
    ]
    sketches = [
        outer_sum(project_rows(grads, projection) * live_rows, inputs_proj)
        for grads, projection, inputs_proj in pairs
    ]
    partial_sum = jnp.stack(sketches, axis=0)[None]
    shared = reduce_positions(partial_sum)
    gathered = lax.all_gather(shared, "dp", axis=0, tiled=True)
    return pick_owned(gathered, example_ids)


def solution(mesh):
    return jax.shard_map(
        shards,
        mesh=mesh,
        in_specs=(
            P("dp", "ctx", None),
            P("dp", "ctx", None),
            P("dp", "ctx", None),
            P("dp", "ctx", None),
            P("dp", "ctx", None),
            P("dp", "ctx", None),
            P("dp", "ctx", None),
            P("dp", "ctx", None),
            P("dp", "ctx", None),
            P("dp", "ctx", None),
            P("dp", "ctx", None),
            P(),
            P(),
            P(),
            P(),
            P(),
            P(),
            P(),
            P(),
            P(),
            P(),
            P(),
            P("dp"),
            P(),
        ),
        out_specs=P("dp", None, "ctx"),
        check_vma=False,
    )
```

profile of v0, /device:TPU:1, one launch (start us, length us, event | category | flops | bytes accessed | tf_op | source)
XLA Modules:
  0.0 140.8 jit_solution(12949452242620769150)
XLA Ops:
  6.5 0.0 copy-start
  6.5 0.0 all-reduce.2.cloned.1.call-start
  7.3 1.8 %convolution_convert_fusion.6 = bf16[128,64]{0,1:T(8,128)(2,1)S(1)} fusion(bf16[4096,64]{0,1:T(8,128)(2,1)} %param.37, bf16[1,128,4096]{2,1,0:T(8,128)(2,1)} %param.26), kind=kOutput, calls=%fused_computation.29 | convolution fusion | flops 67117056 | bytes 1589248 | tf_op jit(solution)/shard_map/dot_general | solution.py:8
  9.2 0.0 copy-done
  9.2 3.3 %fusion.22 = f32[64,64]{1,0:T(8,128)S(1)} fusion(bf16[128,64]{0,1:T(8,128)(2,1)S(1)} %convolution_convert_fusion.6, bf16[14336,64]{0,1:T(8,128)(2,1)S(1)} %copy-done, bf16[1,128,14336]{2,1,0:T(8,128)(2,1)} %param.33, bf16[128]{0:T(256)(128)(2,1)S(1)} %compare_convert_fusion), kind=kOutput, calls=%fused_computation.17 | convolution fusion | flops 235945984 | bytes 5538048 | tf_op jit(solution)/shard_map/dot_general | solution.py:12
  12.5 0.1 stack_reshape.26
  12.6 0.0 copy-start.1
  12.6 4.0 %fusion.28 = f32[64,64]{1,0:T(8,128)S(1)} fusion(bf16[128,64]{0,1:T(8,128)(2,1)S(1)} %convolution_convert_fusion.6, bf16[14336,64]{0,1:T(8,128)(2,1)} %param.43, bf16[1,128,14336]{2,1,0:T(8,128)(2,1)} %param.32, bf16[128]{0:T(256)(128)(2,1)S(1)} %compare_convert_fusion), kind=kOutput, calls=%fused_computation.19 | convolution fusion | flops 235945984 | bytes 5538048 | tf_op jit(solution)/shard_map/dot_general | solution.py:12
  16.6 0.1 stack_reshape.25
  16.7 1.7 %convolution_convert_fusion.7 = bf16[128,64]{0,1:T(8,128)(2,1)S(1)} fusion(bf16[4096,64]{0,1:T(8,128)(2,1)S(1)} %copy-done.2, bf16[1,128,4096]{2,1,0:T(8,128)(2,1)} %param.24), kind=kOutput, calls=%fused_computation.30 | convolution fusion | flops 67117056 | bytes 1589248 | tf_op jit(solution)/shard_map/dot_general | solution.py:8
  18.4 0.0 copy-start.3
  18.4 1.4 %fusion.38 = f32[64,64]{1,0:T(8,128)S(1)} fusion(bf16[128,64]{0,1:T(8,128)(2,1)S(1)} %convolution_convert_fusion.7, bf16[1024,64]{0,1:T(8,128)(2,1)} %param.41, bf16[1,128,1024]{2,1,0:T(8,128)(2,1)} %param.30, bf16[128]{0:T(256)(128)(2,1)S(1)} %compare_convert_fusion), kind=kOutput, calls=%fused_computation.28 | convolution fusion | flops 17842176 | bytes 426240 | tf_op jit(solution)/shard_map/dot_general | solution.py:12
  19.8 0.1 stack_reshape.23
  20.0 1.4 fusion.36
  21.3 0.1 stack_reshape.22
  21.4 1.6 %fusion.31 = f32[64,64]{1,0:T(8,128)S(1)} fusion(bf16[128,64]{0,1:T(8,128)(2,1)S(1)} %convolution_convert_fusion.7, bf16[4096,64]{0,1:T(8,128)(2,1)} %param.39, bf16[1,128,4096]{2,1,0:T(8,128)(2,1)S(1)} %copy-done.1, bf16[128]{0:T(256)(128)(2,1)S(1)} %compare_convert_fusion), kind=kOutput, calls=%fused_computation.21 | convolution fusion | flops 68173824 | bytes 1605888 | tf_op jit(solution)/shard_map/dot_general | solution.py:12
  23.1 0.1 stack_reshape.21
  23.2 1.8 %convolution_convert_fusion.1 = bf16[128,64]{1,0:T(8,128)(2,1)S(1)} fusion(bf16[4096,64]{0,1:T(8,128)(2,1)} %param.36, bf16[1,128,4096]{2,1,0:T(8,128)(2,1)} %param.25), kind=kOutput, calls=%fused_computation.10 | convolution fusion | flops 67117056 | bytes 1589248 | tf_op jit(solution)/shard_map/dot_general | solution.py:8
  25.0 0.0 copy-done.3
  25.0 1.8 %fusion.33 = f32[64,64]{1,0:T(8,128)S(1)} fusion(bf16[128,64]{1,0:T(8,128)(2,1)S(1)} %convolution_convert_fusion.1, bf16[4096,64]{0,1:T(8,128)(2,1)S(1)} %copy-done.3, bf16[1,128,4096]{2,1,0:T(8,128)(2,1)} %param.31, bf16[128]{0:T(256)(128)(2,1)S(1)} %compare_convert_fusion), kind=kOutput, calls=%fused_computation.23 | convolution fusion | flops 68173824 | bytes 1605888 | tf_op jit(solution)/shard_map/dot_general | solution.py:12
  26.8 0.1 stack_reshape.24
  26.9 0.0 copy-start.4
  26.9 1.8 %fusion.34 = bf16[128,64]{1,0:T(8,128)(2,1)S(1)} fusion(bf16[4096,64]{0,1:T(8,128)(2,1)} %param.45, bf16[1,128,4096]{2,1,0:T(8,128)(2,1)} %param.34, bf16[128]{0:T(256)(128)(2,1)S(1)} %compare_convert_fusion), kind=kOutput, calls=%fused_computation.24 | convolution fusion | flops 67125248 | bytes 1589504 | tf_op jit(solution)/shard_map/dot_general | solution.py:8
  28.7 3.8 %fusion.16 = f32[64,64]{1,0:T(8,128)S(1)} fusion(bf16[128,64]{1,0:T(8,128)(2,1)S(1)} %fusion.34, bf16[14336,64]{0,1:T(8,128)(2,1)} %param.38, bf16[1,128,14336]{2,1,0:T(8,128)(2,1)} %param.27), kind=kOutput, calls=%fused_computation.15 | convolution fusion | flops 235937792 | bytes 5537792 | tf_op jit(solution)/shard_map/dot_general | solution.py:12
  32.5 0.1 stack_reshape.27
  32.6 0.8 stack.3
  33.4 0.0 all-reduce.2.cloned.1.call-update
  33.5 83.8 %all-reduce.2.cloned.1.call-done = f32[1,7,4096]{2,1,0:T(8,128)} async-done(((f32[1,7,4096]{2,1,0:T(8,128)}), f32[1,7,4096]{2,1,0:T(8,128)}) %all-reduce.2.cloned.1.call-update) | async-done | bytes 114704 | tf_op jit(solution)/shard_map/psum | solution.py:19
  117.3 0.7 constant_dynamic-slice_fusion
  118.0 15.2 %all_gather.3 = f32[8,7,256]{2,1,0:T(8,128)S(1)} all-gather(f32[1,7,256]{2,1,0:T(8,128)S(1)} %constant_dynamic-slice_fusion), channel_id=1, replica_groups=mesh['dp'=8,'ctx'=16] {'dp'}, dimensions={0}, use_global_device_ids=true | all-gather | bytes 64512 | tf_op jit(solution)/shard_map/all_gather | solution.py:81
  133.3 0.1 multiply_reduce_fusion
  133.3 0.6 broadcast_in_dim.9
  (6 shorter events, 0.0 us)
Async XLA Ops:
  6.5 2.7 %copy-start = (bf16[14336,64]{0,1:T(8,128)(2,1)S(1)}, bf16[14336,64]{0,1:T(8,128)(2,1)}, u32[]{:S(2)}) copy-start(bf16[14336,64]{0,1:T(8,128)(2,1)} %param.44) | copy-start | bytes 5505028
  6.5 110.8 %all-reduce.2.cloned.1.call-start = ((), (), s32[]{:S(2)}) async-start(), calls=%async_computation | async-start | bytes 262144 | tf_op jit(solution)/shard_map/psum | solution.py:19
  12.5 4.2 %copy-start.2 = (bf16[4096,64]{0,1:T(8,128)(2,1)S(1)}, bf16[4096,64]{0,1:T(8,128)(2,1)}, u32[]{:S(2)}) copy-start(bf16[4096,64]{0,1:T(8,128)(2,1)} %param.35) | copy-start | bytes 1572868
  12.6 8.8 %copy-start.1 = (bf16[1,128,4096]{2,1,0:T(8,128)(2,1)S(1)}, bf16[1,128,4096]{2,1,0:T(8,128)(2,1)}, u32[]{:S(2)}) copy-start(bf16[1,128,4096]{2,1,0:T(8,128)(2,1)} %param.28) | copy-start | bytes 3145732
  18.4 6.6 %copy-start.3 = (bf16[4096,64]{0,1:T(8,128)(2,1)S(1)}, bf16[4096,64]{0,1:T(8,128)(2,1)}, u32[]{:S(2)}) copy-start(bf16[4096,64]{0,1:T(8,128)(2,1)} %param.42) | copy-start | bytes 1572868
  26.9 6.6 %copy-start.4 = (s32[8]{0:T(128)S(1)}, s32[8]{0:T(128)}, u32[]{:S(2)}) copy-start(s32[8]{0:T(128)} %param.47) | copy-start | bytes 100
Sparse Core Ops, SparseCore 0:
  33.6 83.6 all-reduce.1
where the time goes:
time: 141 us
  waiting for transfers between devices  83.8 us (59%)
  matrix products  24.4 us (17%)
  blocking collectives  15.2 us (11%)
  between operations  14.3 us (10%)
  local copies, waits for them, and re-layouts  2.84 us (2%)
    psum x1, waiting for transfers between devices, reduce_positions(): summed = lax.psum(values, 'ctx')  83.8 us
    dot_general x7, matrix products, outer_sum(): lax.dot_general(grads_proj, inputs_proj, (((0,), (0,)), ((), ())), prefer...  17.3 us
    all_gather x1, blocking collectives, shards(): gathered = lax.all_gather(shared, 'dp', axis=0, tiled=True)  15.2 us
    dot_general x4, matrix products, project_rows(): jnp.dot(acts[0], projection, preferred_element_type=jnp.float32)  7.1 us
  transfers between devices with their start and end apart: 1, of which 1 were waited for; matrix products, arithmetic and copies ran while one was open for 0% of the time, Pallas kernels for 0%

commit v1 on v0

v1 whole, which is shorter than its diff:
```python
import functools

import jax
import jax.numpy as jnp
from jax import lax
from jax.experimental import pallas as pl
from jax.experimental.pallas import tpu as pltpu
from jax.sharding import PartitionSpec as P

RANK = 64
PIECES = 16
CHUNK = 2048
GROUPS = (
    ("attn_in", ("grad_query", "grad_key", "grad_value")),
    ("attn_mix", ("grad_output",)),
    ("mlp_in", ("grad_gate", "grad_up")),
    ("mlp_act", ("grad_down",)),
)
PROJ = {
    "attn_in": "proj_attn",
    "attn_mix": "proj_mix",
    "mlp_in": "proj_mlp",
    "mlp_act": "proj_act",
    "grad_query": "proj_query",
    "grad_key": "proj_key",
    "grad_value": "proj_value",
    "grad_output": "proj_output",
    "grad_gate": "proj_gate",
    "grad_up": "proj_upward",
    "grad_down": "proj_down",
}
MAPS = ("grad_query", "grad_key", "grad_value", "grad_output", "grad_gate", "grad_up", "grad_down")
ORDER = tuple(name for first, rest in GROUPS for name in (first, *rest))
NAMES = (
    "attn_in", "attn_mix", "mlp_in", "mlp_act",
    "grad_query", "grad_key", "grad_value", "grad_output", "grad_gate", "grad_up", "grad_down",
    "proj_attn", "proj_mix", "proj_mlp", "proj_act",
    "proj_query", "proj_key", "proj_value", "proj_output", "proj_gate", "proj_upward", "proj_down",
    "seq_counts", "example_ids",
)


def sketch_kernel(widths, *refs):
    n = len(ORDER)
    counts = refs[0]
    acts = dict(zip(ORDER, refs[1 : 1 + n]))
    projs = dict(zip(ORDER, refs[1 + n : 1 + 2 * n]))
    out = refs[1 + 2 * n]
    act_bufs = dict(zip(ORDER, refs[2 + 2 * n : 2 + 3 * n]))
    proj_bufs = dict(zip(ORDER, refs[2 + 3 * n : 2 + 4 * n]))
    square, act_sem, proj_sem = refs[2 + 4 * n :]
    rows = act_bufs[ORDER[0]].shape[0]

    copies = {}
    slot = 0
    for name in ORDER:
        for start in range(0, widths[name], CHUNK):
            part = pl.ds(start, min(CHUNK, widths[name] - start))
            copies[name, start] = (
                pltpu.make_async_copy(
                    projs[name].at[:, part], proj_bufs[name].at[:, part], proj_sem.at[slot]
                ),
                pltpu.make_async_copy(
                    acts[name].at[0, :, part], act_bufs[name].at[:, part], act_sem.at[slot]
                ),
            )
            for copy in copies[name, start]:
                copy.start()
            slot += 1

    def project(name):
        total = None
        for start in range(0, widths[name], CHUNK):
            part = pl.ds(start, min(CHUNK, widths[name] - start))
            for copy in copies[name, start]:
                copy.wait()
            product = lax.dot_general(
                act_bufs[name][:, part],
                proj_bufs[name][:, part],
                (((1,), (1,)), ((), ())),
                preferred_element_type=jnp.float32,
            )
            total = product if total is None else total + product
        return total

    first_pos = lax.axis_index("ctx") * rows
    position = first_pos + lax.broadcasted_iota(jnp.int32, (rows, RANK), 0)
    live = position < counts[0]
    for first, rest in GROUPS:
        inputs_proj = project(first).astype(jnp.bfloat16)
        for name in rest:
            at = MAPS.index(name)
            grads_proj = jnp.where(live, project(name), 0.0).astype(jnp.bfloat16)
            square[at] = lax.dot_general(
                grads_proj,
                inputs_proj,
                (((0,), (0,)), ((), ())),
                preferred_element_type=jnp.float32,
            )
            step = RANK // PIECES
            lanes = [square[at, pl.ds(k, PIECES, stride=step), :] for k in range(step)]
            out[:, at, :] = jnp.concatenate(lanes, axis=1)


def sketches(values):
    widths = {name: values[name].shape[2] for name in ORDER}
    rows = values["attn_in"].shape[1]
    slots = sum(-(-width // CHUNK) for width in widths.values())
    hbm = pl.BlockSpec(memory_space=pl.ANY)
    total = sum(widths.values())
    return pl.pallas_call(
        functools.partial(sketch_kernel, widths),
        out_shape=jax.ShapeDtypeStruct((PIECES, len(MAPS), RANK * RANK // PIECES), jnp.float32),
        in_specs=[pl.BlockSpec(memory_space=pltpu.SMEM)] + [hbm] * (2 * len(ORDER)),
        out_specs=pl.BlockSpec(memory_space=pltpu.VMEM),
        scratch_shapes=[
            *[pltpu.VMEM((rows, widths[name]), jnp.bfloat16) for name in ORDER],
            *[pltpu.VMEM((RANK, widths[name]), jnp.bfloat16) for name in ORDER],
            pltpu.VMEM((len(MAPS), RANK, RANK), jnp.float32),
            pltpu.SemaphoreType.DMA((slots,)),
            pltpu.SemaphoreType.DMA((slots,)),
        ],
        compiler_params=pltpu.CompilerParams(vmem_limit_bytes=60 * 1024 * 1024),
        cost_estimate=pl.CostEstimate(
            flops=2 * rows * RANK * total, bytes_accessed=2 * (rows + RANK) * total, transcendentals=0
        ),
    )(
        values["seq_counts"],
        *[values[name] for name in ORDER],
        *[values[PROJ[name]].T for name in ORDER],
    )


def shards(*args):
    values = dict(zip(NAMES, args))
    pieces = sketches(values)
    pieces = lax.all_to_all(pieces, "ctx", 0, 0, tiled=True)
    own = jnp.sum(pieces, axis=0)
    groups = lax.axis_size("dp")
    target = values["example_ids"][lax.axis_index("dp")]
    chosen = jnp.arange(groups, dtype=jnp.int32) == target
    spread = jnp.where(chosen[:, None, None], own[None], 0.0)
    arrived = lax.all_to_all(spread, "dp", 0, 0, tiled=True)
    return jnp.sum(arrived, axis=0, keepdims=True)


def solution(mesh):
    split = P("dp", "ctx", None)
    return jax.shard_map(
        shards,
        mesh=mesh,
        in_specs=(*[split] * 11, *[P()] * 11, P("dp"), P()),
        out_specs=P("dp", None, "ctx"),
        check_vma=False,
    )
```

time: 141 us -> 43.6 us (0.31)
  waiting for transfers between devices: 83.8 us -> 5.61 us
  matrix products: 24.4 us -> 0 us
  Pallas kernels: 0 us -> 15.5 us
  between operations: 14.3 us -> 0.7 us
  starting transfers between devices: 0.01 us -> 7.6 us
  blocking collectives: 15.2 us -> 12 us
  local copies, waits for them, and re-layouts: 2.84 us -> 1.19 us
    psum x1 -> x0, waiting for transfers between devices: 83.8 us -> none  [reduce_positions(): summed = lax.psum(values, 'ctx')]
    dot_general x11 -> x0, matrix products: 24.4 us -> none  [the longest x7 17.3 us: outer_sum(): lax.dot_general(grads_proj, inputs_proj, (((0,), (0,)), ((), ())), prefer...]
    pallas_call x0 -> x1, Pallas kernels: none -> 15.5 us  [sketches(): pl.pallas_call(functools.partial(sketch_kernel, widths), out_shape=jax.Sh...]
    all_gather x1 -> x0, blocking collectives: 15.2 us -> none  [shards(): gathered = lax.all_gather(shared, 'dp', axis=0, tiled=True)]
    all_to_all x0 -> x1, blocking collectives: none -> 12 us  [shards(): arrived = lax.all_to_all(spread, 'dp', 0, 0, tiled=True)]
    all_to_all x0 -> x1, starting transfers between devices: none -> 7.6 us  [shards(): pieces = lax.all_to_all(pieces, 'ctx', 0, 0, tiled=True)]
    all_to_all x0 -> x1, waiting for transfers between devices: none -> 5.61 us  [shards(): pieces = lax.all_to_all(pieces, 'ctx', 0, 0, tiled=True)]
    another operation x8 -> x0, local copies, waits for them, and re-layouts: 1.51 us -> none  [shards(): partial_sum = jnp.stack(sketches, axis=0)[None]]
  transfers between devices with their start and end apart: 1 -> 1, of which waited for: 1 -> 1; matrix products, arithmetic and copies ran while one was open for 0% -> 3% of each run, Pallas kernels for 0% -> 0%
where the time goes in v1:
time: 43.6 us; the launch traced here: 43.4 us
  Pallas kernels  15.5 us (36%)
  blocking collectives  12 us (28%)
  starting transfers between devices  7.6 us (17%)
  waiting for transfers between devices  5.61 us (13%)
  local copies, waits for them, and re-layouts  1.19 us (3%)
  other arithmetic  0.76 us (2%)
  between operations  0.7 us (2%)
    pallas_call x1, Pallas kernels, sketches(): pl.pallas_call(functools.partial(sketch_kernel, widths), out_shape=jax.Sh...  15.5 us
    all_to_all x1, blocking collectives, shards(): arrived = lax.all_to_all(spread, 'dp', 0, 0, tiled=True)  12 us
    all_to_all x1, starting transfers between devices, shards(): pieces = lax.all_to_all(pieces, 'ctx', 0, 0, tiled=True)  7.6 us
    all_to_all x1, waiting for transfers between devices, shards(): pieces = lax.all_to_all(pieces, 'ctx', 0, 0, tiled=True)  5.61 us
  transfers between devices with their start and end apart: 1, of which 1 were waited for; matrix products, arithmetic and copies ran while one was open for 3% of the time, Pallas kernels for 0%

profile of v1, /device:TPU:1, one launch (start us, length us, event | category | flops | bytes accessed | tf_op | source)
XLA Modules:
  0.0 43.4 jit_solution(14579347740289055662)
XLA Ops:
  0.7 0.0 copy-start
  0.7 15.5 %shard_map.226 = f32[16,7,256]{2,1,0:T(8,128)} custom-call(s32[1]{0:T(128)S(6)} %copy.29.refs_0_, bf16[1,128,4096]{2,1,0:T(8,128)(2,1)} %refs_1_.1, bf16[1,128,4096]{2,1,0:T(8,128)(2,1)} %refs_2_.1, bf16[1,128,1024]{2,1,0:T(8,128)(2,1)} %refs_3_.1, bf16[1,128,1024]{2,1,0:T(8,128)(2,1)} %refs_4_.1, bf16[1,128,4096]{2,1,0:T(8,128)(2,1)} %refs_5_.1, ...), custom_call_target="tpu_custom_call" | custom-call | flops 1140850688 | bytes 26738688 | tf_op jit(solution)/shard_map/pallas_call | solution.py:111
  16.2 7.6 %all-to-all-start = ((f32[16,7,256]{2,1,0:T(8,128)}), f32[16,7,256]{2,1,0:T(8,128)S(1)}, u32[]{:S(2)}, u32[]{:S(2)}) async-start(f32[16,7,256]{2,1,0:T(8,128)} %shard_map.226), calls=%async_computation | async-start | bytes 262144 | tf_op jit(solution)/shard_map/all_to_all | solution.py:137
  23.8 0.0 copy-done
  23.8 0.6 %dynamic_slice.3 = s32[1]{0:T(128)} dynamic-slice(s32[8]{0:T(128)S(1)} %copy-done, s32[]{:T(128)S(6)} %select_n.7), dynamic_slice_sizes={1} | dynamic-slice | bytes 12 | tf_op jit(solution)/shard_map/dynamic_slice | solution.py:140
  24.4 0.6 %iota_compare_fusion = pred[8]{0:T(512)(128)(4,1)S(1)} fusion(s32[]{:T(128)} %bitcast), kind=kLoop, calls=%fused_computation.1 | loop fusion | flops 8 | bytes 12 | tf_op jit(solution)/shard_map/eq | solution.py:141
  25.0 5.6 %all-to-all-done = f32[16,7,256]{2,1,0:T(8,128)S(1)} async-done(((f32[16,7,256]{2,1,0:T(8,128)}), f32[16,7,256]{2,1,0:T(8,128)S(1)}, u32[]{:S(2)}, u32[]{:S(2)}) %all-to-all-start) | async-done | bytes 114720 | tf_op jit(solution)/shard_map/all_to_all | solution.py:137
  30.7 0.1 broadcast_select_fusion
  30.7 12.0 %all_to_all.10 = f32[8,7,256]{2,1,0:T(8,128)S(1)} all-to-all(f32[8,7,256]{2,1,0:T(8,128)S(1)} %broadcast_select_fusion), channel_id=1, replica_groups=mesh['dp'=8,'ctx'=16] {'dp'}, dimensions={0} | all-to-all | bytes 114688 | tf_op jit(solution)/shard_map/all_to_all | solution.py:143
  42.8 0.6 %copy.27 = f32[1,7,256]{2,0,1:T(1,128)} copy(f32[1,7,256]{2,1,0:T(8,128)S(1)} %bitcast.24) | data formatting | bytes 14336 | tf_op jit(solution)/shard_map/broadcast_in_dim | solution.py:144
  (2 shorter events, 0.0 us)
Async XLA Ops:
  0.7 23.1 %copy-start = (s32[8]{0:T(128)S(1)}, s32[8]{0:T(128)}, u32[]{:S(2)}) copy-start(s32[8]{0:T(128)} %param.47) | copy-start | bytes 100
  16.2 14.5 %all-to-all-start = ((f32[16,7,256]{2,1,0:T(8,128)}), f32[16,7,256]{2,1,0:T(8,128)S(1)}, u32[]{:S(2)}, u32[]{:S(2)}) async-start(f32[16,7,256]{2,1,0:T(8,128)} %shard_map.226), calls=%async_computation | async-start | bytes 262144 | tf_op jit(solution)/shard_map/all_to_all | solution.py:137

commit v2 on v1

--- a/solution.py
+++ b/solution.py
@@ -40,6 +40,9 @@
 )
 
 
+SLABS = 4
+
+
 def sketch_kernel(widths, *refs):
     n = len(ORDER)
     counts = refs[0]
@@ -49,42 +52,45 @@
     act_bufs = dict(zip(ORDER, refs[2 + 2 * n : 2 + 3 * n]))
     proj_bufs = dict(zip(ORDER, refs[2 + 3 * n : 2 + 4 * n]))
     square, act_sem, proj_sem = refs[2 + 4 * n :]
-    rows = act_bufs[ORDER[0]].shape[0]
+    rows = acts[ORDER[0]].shape[1]
 
     copies = {}
-    slot = 0
-    for name in ORDER:
-        for start in range(0, widths[name], CHUNK):
-            part = pl.ds(start, min(CHUNK, widths[name] - start))
-            copies[name, start] = (
+    for at, name in enumerate(ORDER):
+        slab = widths[name] // SLABS
+        copies[name] = []
+        for k in range(SLABS):
+            part = pl.ds(k * slab, slab)
+            copies[name] += [
                 pltpu.make_async_copy(
-                    projs[name].at[:, part], proj_bufs[name].at[:, part], proj_sem.at[slot]
+                    projs[name].at[:, part],
+                    proj_bufs[name].at[pl.ds(k * RANK, RANK), :],
+                    proj_sem.at[at * SLABS + k],
                 ),
                 pltpu.make_async_copy(
-                    acts[name].at[0, :, part], act_bufs[name].at[:, part], act_sem.at[slot]
+                    acts[name].at[0, :, part],
+                    act_bufs[name].at[pl.ds(k * rows, rows), :],
+                    act_sem.at[at * SLABS + k],
                 ),
-            )
-            for copy in copies[name, start]:
-                copy.start()
-            slot += 1
+            ]
+        for copy in copies[name]:
+            copy.start()
 
     def project(name):
-        total = None
-        for start in range(0, widths[name], CHUNK):
-            part = pl.ds(start, min(CHUNK, widths[name] - start))
-            for copy in copies[name, start]:
-                copy.wait()
-            product = lax.dot_general(
-                act_bufs[name][:, part],
-                proj_bufs[name][:, part],
-                (((1,), (1,)), ((), ())),
-                preferred_element_type=jnp.float32,
-            )
-            total = product if total is None else total + product
-        return total
+        for copy in copies[name]:
+            copy.wait()
+        product = lax.dot_general(
+            proj_bufs[name][...],
+            act_bufs[name][...],
+            (((1,), (1,)), ((), ())),
+            preferred_element_type=jnp.float32,
+        )
+        blocks = [
+            product[k * RANK : (k + 1) * RANK, k * rows : (k + 1) * rows] for k in range(SLABS)
+        ]
+        return functools.reduce(lambda a, b: a + b, blocks)
 
     first_pos = lax.axis_index("ctx") * rows
-    position = first_pos + lax.broadcasted_iota(jnp.int32, (rows, RANK), 0)
+    position = first_pos + lax.broadcasted_iota(jnp.int32, (RANK, rows), 1)
     live = position < counts[0]
     for first, rest in GROUPS:
         inputs_proj = project(first).astype(jnp.bfloat16)
@@ -94,7 +100,7 @@
             square[at] = lax.dot_general(
                 grads_proj,
                 inputs_proj,
-                (((0,), (0,)), ((), ())),
+                (((1,), (1,)), ((), ())),
                 preferred_element_type=jnp.float32,
             )
             step = RANK // PIECES
@@ -105,7 +111,6 @@
 def sketches(values):
     widths = {name: values[name].shape[2] for name in ORDER}
     rows = values["attn_in"].shape[1]
-    slots = sum(-(-width // CHUNK) for width in widths.values())
     hbm = pl.BlockSpec(memory_space=pl.ANY)
     total = sum(widths.values())
     return pl.pallas_call(
@@ -114,11 +119,11 @@
         in_specs=[pl.BlockSpec(memory_space=pltpu.SMEM)] + [hbm] * (2 * len(ORDER)),
         out_specs=pl.BlockSpec(memory_space=pltpu.VMEM),
         scratch_shapes=[
-            *[pltpu.VMEM((rows, widths[name]), jnp.bfloat16) for name in ORDER],
-            *[pltpu.VMEM((RANK, widths[name]), jnp.bfloat16) for name in ORDER],
+            *[pltpu.VMEM((SLABS * rows, widths[name] // SLABS), jnp.bfloat16) for name in ORDER],
+            *[pltpu.VMEM((SLABS * RANK, widths[name] // SLABS), jnp.bfloat16) for name in ORDER],
             pltpu.VMEM((len(MAPS), RANK, RANK), jnp.float32),
-            pltpu.SemaphoreType.DMA((slots,)),
-            pltpu.SemaphoreType.DMA((slots,)),
+            pltpu.SemaphoreType.DMA((SLABS * len(ORDER),)),
+            pltpu.SemaphoreType.DMA((SLABS * len(ORDER),)),
         ],
         compiler_params=pltpu.CompilerParams(vmem_limit_bytes=60 * 1024 * 1024),
         cost_estimate=pl.CostEstimate(
@@ -131,17 +136,30 @@
     )
 
 
+def route_rows(own, example_ids):
+    groups = lax.axis_size("dp")
+    me = lax.axis_index("dp")
+    slots = jnp.arange(groups, dtype=jnp.int32)
+    held = jnp.bitwise_xor(me, jnp.array([0, 1, 3, 2], jnp.int32))
+    rows = jnp.sum(jnp.where(held[:, None] == slots[None, :], example_ids[None, :], 0), axis=1)
+    keep = (rows == me)[:, None, None]
+    give = (rows == jnp.bitwise_xor(me, 7))[:, None, None]
+
+    def swap(value, flip):
+        return lax.ppermute(value, "dp", [(i, i ^ flip) for i in range(groups)])
+
+    two = jnp.stack([own, swap(own, 1)])
+    four = jnp.concatenate([two, swap(two, 3)])
+    arrived = swap(jnp.sum(jnp.where(give, four, 0.0), axis=0), 7)
+    return (jnp.sum(jnp.where(keep, four, 0.0), axis=0) + arrived)[None]
+
+
 def shards(*args):
     values = dict(zip(NAMES, args))
     pieces = sketches(values)
     pieces = lax.all_to_all(pieces, "ctx", 0, 0, tiled=True)
     own = jnp.sum(pieces, axis=0)
-    groups = lax.axis_size("dp")
-    target = values["example_ids"][lax.axis_index("dp")]
-    chosen = jnp.arange(groups, dtype=jnp.int32) == target
-    spread = jnp.where(chosen[:, None, None], own[None], 0.0)
-    arrived = lax.all_to_all(spread, "dp", 0, 0, tiled=True)
-    return jnp.sum(arrived, axis=0, keepdims=True)
+    return route_rows(own, values["example_ids"])
 
 
 def solution(mesh):

time: 43.6 us -> 39.3 us (0.901)
  blocking collectives: 12 us -> 0 us
  starting transfers between devices: 7.6 us -> 15.6 us
  waiting for transfers between devices: 5.61 us -> 10.2 us
  Pallas kernels: 15.5 us -> 11.6 us
  local copies, waits for them, and re-layouts: 1.19 us -> 0.63 us
    all_to_all x1 -> x0, blocking collectives: 12 us -> none  [shards(): arrived = lax.all_to_all(spread, 'dp', 0, 0, tiled=True)]
    ppermute x0 -> x3, starting transfers between devices: none -> 8.04 us  [swap(): return lax.ppermute(value, 'dp', [(i, i ^ flip) for i in range(groups)])]
    pallas_call x1, Pallas kernels: 15.5 us -> 11.6 us  [sketches(): pl.pallas_call(functools.partial(sketch_kernel, widths), out_shape=jax.Sh...]
    ppermute x0 -> x3, waiting for transfers between devices: none -> 3.37 us  [swap(): return lax.ppermute(value, 'dp', [(i, i ^ flip) for i in range(groups)])]
    all_to_all x1, waiting for transfers between devices: 5.61 us -> 6.84 us  [shards(): pieces = lax.all_to_all(pieces, 'ctx', 0, 0, tiled=True)]
    eq x1, other arithmetic: 0.65 us -> 0.01 us  [route_rows(): keep = (rows == me)[:, None, None]]
    dynamic_slice x1 -> x0, local copies, waits for them, and re-layouts: 0.59 us -> none  [shards(): target = values['example_ids'][lax.axis_index('dp')]]
  transfers between devices with their start and end apart: 1 -> 4, of which waited for: 1 -> 4; matrix products, arithmetic and copies ran while one was open for 3% -> 1% of each run, Pallas kernels for 0% -> 0%
where the time goes in v2:
time: 39.3 us; the launch traced here: 39.1 us
  starting transfers between devices  15.6 us (40%)
  Pallas kernels  11.6 us (30%)
  waiting for transfers between devices  10.2 us (26%)
  between operations  0.72 us (2%)
  local copies, waits for them, and re-layouts  0.63 us (2%)
    pallas_call x1, Pallas kernels, sketches(): pl.pallas_call(functools.partial(sketch_kernel, widths), out_shape=jax.Sh...  11.6 us
    ppermute x3, starting transfers between devices, swap(): return lax.ppermute(value, 'dp', [(i, i ^ flip) for i in range(groups)])  8.04 us
    all_to_all x1, starting transfers between devices, shards(): pieces = lax.all_to_all(pieces, 'ctx', 0, 0, tiled=True)  7.59 us
    all_to_all x1, waiting for transfers between devices, shards(): pieces = lax.all_to_all(pieces, 'ctx', 0, 0, tiled=True)  6.84 us
    ppermute x3, waiting for transfers between devices, swap(): return lax.ppermute(value, 'dp', [(i, i ^ flip) for i in range(groups)])  3.37 us
  transfers between devices with their start and end apart: 4, of which 4 were waited for; matrix products, arithmetic and copies ran while one was open for 1% of the time, Pallas kernels for 0%

profile of v2, /device:TPU:1, one launch (start us, length us, event | category | flops | bytes accessed | tf_op | source)
XLA Modules:
  0.0 39.1 jit_solution(12233045041141289001)
XLA Ops:
  0.7 0.0 copy-start.1
  0.7 0.0 copy-start
  0.7 11.6 %shard_map.235 = f32[16,7,256]{2,1,0:T(8,128)} custom-call(s32[1]{0:T(128)S(6)} %copy.29.refs_0_, bf16[1,128,4096]{2,1,0:T(8,128)(2,1)} %refs_1_.1, bf16[1,128,4096]{2,1,0:T(8,128)(2,1)} %refs_2_.1, bf16[1,128,1024]{2,1,0:T(8,128)(2,1)} %refs_3_.1, bf16[1,128,1024]{2,1,0:T(8,128)(2,1)} %refs_4_.1, bf16[1,128,4096]{2,1,0:T(8,128)(2,1)} %refs_5_.1, ...), custom_call_target="tpu_custom_call" | custom-call | flops 1140850688 | bytes 26738688 | tf_op jit(solution)/shard_map/pallas_call | solution.py:116
  12.3 7.6 %all-to-all-start = ((f32[16,7,256]{2,1,0:T(8,128)}), f32[16,7,256]{2,1,0:T(8,128)S(1)}, u32[]{:S(2)}, u32[]{:S(2)}) async-start(f32[16,7,256]{2,1,0:T(8,128)} %shard_map.235), calls=%async_computation | async-start | bytes 262144 | tf_op jit(solution)/shard_map/all_to_all | solution.py:160
  19.9 0.0 copy-done.1
  19.9 6.8 %all-to-all-done = f32[16,7,256]{2,1,0:T(8,128)S(1)} async-done(((f32[16,7,256]{2,1,0:T(8,128)}), f32[16,7,256]{2,1,0:T(8,128)S(1)}, u32[]{:S(2)}, u32[]{:S(2)}) %all-to-all-start) | async-done | bytes 114720 | tf_op jit(solution)/shard_map/all_to_all | solution.py:160
  26.7 2.2 %collective-permute-start = (f32[7,256]{1,0:T(8,128)S(1)}, f32[7,256]{1,0:T(8,128)S(1)}, u32[]{:S(2)}, u32[]{:S(2)}) collective-permute-start(f32[7,256]{1,0:T(8,128)S(1)} %reduce_sum.37), channel_id=1, source_target_pairs={{0,16},{16,0},{32,48},{48,32},{64,80},{80,64},{96,112},{112,96},{1... | collective-permute-start | bytes 21512 | tf_op jit(solution)/shard_map/ppermute | solution.py:149
  28.9 0.0 copy-done
  28.9 0.2 select_reduce_fusion.2
  29.1 0.6 %collective-permute-done = f32[7,256]{1,0:T(8,128)S(1)} collective-permute-done((f32[7,256]{1,0:T(8,128)S(1)}, f32[7,256]{1,0:T(8,128)S(1)}, u32[]{:S(2)}, u32[]{:S(2)}) %collective-permute-start) | collective-permute-done | bytes 7200 | tf_op jit(solution)/shard_map/ppermute | solution.py:149
  29.8 1.9 %collective-permute-start.1 = (f32[2,7,256]{2,0,1:T(2,128)S(1)}, f32[2,7,256]{2,0,1:T(2,128)S(1)}, u32[]{:S(2)}, u32[]{:S(2)}) collective-permute-start(f32[2,7,256]{2,0,1:T(2,128)S(1)} %pad_maximum_fusion.1), channel_id=1, source_target_pairs={{0,48},{16,32},{32,16},{48,0},{64,112},{80,96},{96,80},{112,64},{1... | collective-permute-start | bytes 43016 | tf_op jit(solution)/shard_map/ppermute | solution.py:149
  31.7 1.4 %collective-permute-done.1 = f32[2,7,256]{2,0,1:T(2,128)S(1)} collective-permute-done((f32[2,7,256]{2,0,1:T(2,128)S(1)}, f32[2,7,256]{2,0,1:T(2,128)S(1)}, u32[]{:S(2)}, u32[]{:S(2)}) %collective-permute-start.1) | collective-permute-done | bytes 14368 | tf_op jit(solution)/shard_map/ppermute | solution.py:149
  33.1 0.1 select_reduce_fusion
  33.2 3.9 %collective-permute-start.2 = (f32[7,256]{1,0:T(8,128)S(1)}, f32[7,256]{1,0:T(8,128)S(1)}, u32[]{:S(2)}, u32[]{:S(2)}) collective-permute-start(f32[7,256]{1,0:T(8,128)S(1)} %get-tuple-element.5), channel_id=1, source_target_pairs={{0,112},{16,96},{32,80},{48,64},{64,48},{80,32},{96,16},{112,0},{1... | collective-permute-start | bytes 21512 | tf_op jit(solution)/shard_map/ppermute | solution.py:149
  37.2 1.3 %collective-permute-done.2 = f32[7,256]{1,0:T(8,128)S(1)} collective-permute-done((f32[7,256]{1,0:T(8,128)S(1)}, f32[7,256]{1,0:T(8,128)S(1)}, u32[]{:S(2)}, u32[]{:S(2)}) %collective-permute-start.2) | collective-permute-done | bytes 7200 | tf_op jit(solution)/shard_map/ppermute | solution.py:149
  38.5 0.6 %copy.28 = f32[1,7,256]{2,0,1:T(1,128)} copy(f32[1,7,256]{2,1,0:T(8,128)S(1)} %add_bitcast_fusion) | data formatting | bytes 14336 | tf_op jit(solution)/shard_map/broadcast_in_dim | solution.py:154
  (7 shorter events, 0.1 us)
Async XLA Ops:
  0.7 19.2 %copy-start.1 = (s32[4]{0:T(128)S(1)}, s32[4]{0:T(128)}, u32[]{:S(2)}) copy-start(s32[4]{0:T(128)} %constant.14.clone) | copy-start | bytes 52
  0.7 28.2 %copy-start = (s32[8]{0:T(128)S(1)}, s32[8]{0:T(128)}, u32[]{:S(2)}) copy-start(s32[8]{0:T(128)} %param.48) | copy-start | bytes 100
  12.3 14.5 %all-to-all-start = ((f32[16,7,256]{2,1,0:T(8,128)}), f32[16,7,256]{2,1,0:T(8,128)S(1)}, u32[]{:S(2)}, u32[]{:S(2)}) async-start(f32[16,7,256]{2,1,0:T(8,128)} %shard_map.235), calls=%async_computation | async-start | bytes 262144 | tf_op jit(solution)/shard_map/all_to_all | solution.py:160
  26.7 3.0 %collective-permute-start = (f32[7,256]{1,0:T(8,128)S(1)}, f32[7,256]{1,0:T(8,128)S(1)}, u32[]{:S(2)}, u32[]{:S(2)}) collective-permute-start(f32[7,256]{1,0:T(8,128)S(1)} %reduce_sum.37), channel_id=1, source_target_pairs={{0,16},{16,0},{32,48},{48,32},{64,80},{80,64},{96,112},{112,96},{1... | collective-permute-start | bytes 21512 | tf_op jit(solution)/shard_map/ppermute | solution.py:149
  29.8 3.3 %collective-permute-start.1 = (f32[2,7,256]{2,0,1:T(2,128)S(1)}, f32[2,7,256]{2,0,1:T(2,128)S(1)}, u32[]{:S(2)}, u32[]{:S(2)}) collective-permute-start(f32[2,7,256]{2,0,1:T(2,128)S(1)} %pad_maximum_fusion.1), channel_id=1, source_target_pairs={{0,48},{16,32},{32,16},{48,0},{64,112},{80,96},{96,80},{112,64},{1... | collective-permute-start | bytes 43016 | tf_op jit(solution)/shard_map/ppermute | solution.py:149
  33.2 5.3 %collective-permute-start.2 = (f32[7,256]{1,0:T(8,128)S(1)}, f32[7,256]{1,0:T(8,128)S(1)}, u32[]{:S(2)}, u32[]{:S(2)}) collective-permute-start(f32[7,256]{1,0:T(8,128)S(1)} %get-tuple-element.5), channel_id=1, source_target_pairs={{0,112},{16,96},{32,80},{48,64},{64,48},{80,32},{96,16},{112,0},{1... | collective-permute-start | bytes 21512 | tf_op jit(solution)/shard_map/ppermute | solution.py:149

commit v3 on v2

v3 whole, which is shorter than its diff:
```python
import functools

import jax
import jax.numpy as jnp
from jax import lax
from jax.experimental import pallas as pl
from jax.experimental.pallas import tpu as pltpu
from jax.sharding import PartitionSpec as P

RANK = 64
PIECES = 16
GROUPS = (
    ("attn_in", ("grad_query", "grad_key", "grad_value",)),
    ("attn_mix", ("grad_output",)),
    ("mlp_in", ("grad_gate", "grad_up",)),
    ("mlp_act", ("grad_down",)),
)
PROJ = {
    "attn_in": "proj_attn",
    "attn_mix": "proj_mix",
    "mlp_in": "proj_mlp",
    "mlp_act": "proj_act",
    "grad_query": "proj_query",
    "grad_key": "proj_key",
    "grad_value": "proj_value",
    "grad_output": "proj_output",
    "grad_gate": "proj_gate",
    "grad_up": "proj_upward",
    "grad_down": "proj_down",
}
MAPS = ("grad_query", "grad_key", "grad_value", "grad_output", "grad_gate", "grad_up", "grad_down")
ORDER = tuple(name for first, rest in GROUPS for name in (first, *rest))
NAMES = (
    "attn_in", "attn_mix", "mlp_in", "mlp_act",
    "grad_query", "grad_key", "grad_value", "grad_output", "grad_gate", "grad_up", "grad_down",
    "proj_attn", "proj_mix", "proj_mlp", "proj_act",
    "proj_query", "proj_key", "proj_value", "proj_output", "proj_gate", "proj_upward", "proj_down",
    "seq_counts", "example_ids",
)


SLABS = 4


def sketch_kernel(widths, *refs):
    n = len(ORDER)
    acts = dict(zip(ORDER, refs[:n]))
    projs = dict(zip(ORDER, refs[n : 2 * n]))
    out = refs[2 * n]
    act_bufs = dict(zip(ORDER, refs[1 + 2 * n : 1 + 3 * n]))
    proj_bufs = dict(zip(ORDER, refs[1 + 3 * n : 1 + 4 * n]))
    square, act_sem, proj_sem = refs[1 + 4 * n :]
    rows = acts[ORDER[0]].shape[1]

    copies = {
        name: (
            pltpu.make_async_copy(projs[name], proj_bufs[name], proj_sem.at[k]),
            pltpu.make_async_copy(acts[name].at[0], act_bufs[name], act_sem.at[k]),
        )
        for k, name in enumerate(ORDER)
    }
    for name in ORDER:
        for copy in copies[name]:
            copy.start()

    def project(name):
        for copy in copies[name]:
            copy.wait()
        slab = widths[name] // SLABS
        parts = [pl.ds(k * slab, slab) for k in range(SLABS)]
        product = lax.dot_general(
            jnp.concatenate([proj_bufs[name][:, part] for part in parts], axis=0),
            jnp.concatenate([act_bufs[name][:, part] for part in parts], axis=0),
            (((1,), (1,)), ((), ())),
            preferred_element_type=jnp.float32,
        )
        blocks = [
            product[k * RANK : (k + 1) * RANK, k * rows : (k + 1) * rows] for k in range(SLABS)
        ]
        return functools.reduce(jnp.add, blocks).astype(jnp.bfloat16)

    for first, rest in GROUPS:
        inputs_proj = project(first)
        grads_proj = [project(name) for name in rest]
        at = MAPS.index(rest[0]) * RANK
        size = len(rest) * RANK
        square[pl.ds(at, size), :] = lax.dot_general(
            jnp.concatenate(grads_proj, axis=0),
            inputs_proj,
            (((1,), (1,)), ((), ())),
            preferred_element_type=jnp.float32,
        )
        step = RANK // PIECES
        for name in rest:
            at = MAPS.index(name)
            lanes = [square[pl.ds(at * RANK + k, PIECES, stride=step), :] for k in range(step)]
            out[:, at, :] = jnp.concatenate(lanes, axis=1)


def sketches(values):
    widths = {name: values[name].shape[2] for name in ORDER}
    rows = values["attn_in"].shape[1]
    hbm = pl.BlockSpec(memory_space=pl.ANY)
    total = sum(widths.values())
    return pl.pallas_call(
        functools.partial(sketch_kernel, widths),
        out_shape=jax.ShapeDtypeStruct((PIECES, len(MAPS), RANK * RANK // PIECES), jnp.float32),
        in_specs=[hbm] * (2 * len(ORDER)),
        out_specs=pl.BlockSpec(memory_space=pltpu.VMEM),
        scratch_shapes=[
            *[pltpu.VMEM((rows, widths[name]), jnp.bfloat16) for name in ORDER],
            *[pltpu.VMEM((RANK, widths[name]), jnp.bfloat16) for name in ORDER],
            pltpu.VMEM((len(MAPS) * RANK, RANK), jnp.float32),
            pltpu.SemaphoreType.DMA((len(ORDER),)),
            pltpu.SemaphoreType.DMA((len(ORDER),)),
        ],
        compiler_params=pltpu.CompilerParams(vmem_limit_bytes=60 * 1024 * 1024),
        cost_estimate=pl.CostEstimate(
            flops=2 * rows * RANK * total, bytes_accessed=2 * (rows + RANK) * total, transcendentals=0
        ),
    )(
        *[values[name] for name in ORDER],
        *[values[PROJ[name]].T for name in ORDER],
    )


def route_rows(own, example_ids):
    groups = lax.axis_size("dp")
    me = lax.axis_index("dp")
    slots = jnp.arange(groups, dtype=jnp.int32)
    held = jnp.bitwise_xor(me, jnp.array([0, 1, 3, 2], jnp.int32))
    rows = jnp.sum(jnp.where(held[:, None] == slots[None, :], example_ids[None, :], 0), axis=1)
    keep = (rows == me)[:, None, None]
    give = (rows == jnp.bitwise_xor(me, 7))[:, None, None]

    def swap(value, flip):
        return lax.ppermute(value, "dp", [(i, i ^ flip) for i in range(groups)])

    two = jnp.stack([own, swap(own, 1)])
    four = jnp.concatenate([two, swap(two, 3)])
    arrived = swap(jnp.sum(jnp.where(give, four, 0.0), axis=0), 7)
    return (jnp.sum(jnp.where(keep, four, 0.0), axis=0) + arrived)[None]


def shards(*args):
    values = dict(zip(NAMES, args))
    pieces = sketches(values)
    pieces = lax.all_to_all(pieces, "ctx", 0, 0, tiled=True)
    block = values["attn_in"].shape[1]
    firsts = jnp.arange(pieces.shape[0], dtype=jnp.int32) * block
    live = firsts < values["seq_counts"][0]
    own = jnp.sum(jnp.where(live[:, None, None], pieces, 0.0), axis=0)
    return route_rows(own, values["example_ids"])


def solution(mesh):
    split = P("dp", "ctx", None)
    return jax.shard_map(
        shards,
        mesh=mesh,
        in_specs=(*[split] * 11, *[P()] * 11, P("dp"), P()),
        out_specs=P("dp", None, "ctx"),
        check_vma=False,
    )
```

time: 39.3 us -> 38.1 us (0.969)
  waiting for transfers between devices: 10.2 us -> 9.55 us
  Pallas kernels: 11.6 us -> 11 us
    all_to_all x1, waiting for transfers between devices: 6.84 us -> 6.18 us  [shards(): pieces = lax.all_to_all(pieces, 'ctx', 0, 0, tiled=True)]
    pallas_call x1, Pallas kernels: 11.6 us -> 11 us  [sketches(): pl.pallas_call(functools.partial(sketch_kernel, widths), out_shape=jax.Sh...]
where the time goes in v3:
time: 38.1 us; the launch traced here: 37.9 us
  starting transfers between devices  15.6 us (41%)
  Pallas kernels  11 us (29%)
  waiting for transfers between devices  9.55 us (25%)
  between operations  0.71 us (2%)
  local copies, waits for them, and re-layouts  0.63 us (2%)
  other arithmetic  0.41 us (1%)
    pallas_call x1, Pallas kernels, sketches(): pl.pallas_call(functools.partial(sketch_kernel, widths), out_shape=jax.Sh...  11 us
    ppermute x3, starting transfers between devices, swap(): return lax.ppermute(value, 'dp', [(i, i ^ flip) for i in range(groups)])  8.04 us
    all_to_all x1, starting transfers between devices, shards(): pieces = lax.all_to_all(pieces, 'ctx', 0, 0, tiled=True)  7.6 us
    all_to_all x1, waiting for transfers between devices, shards(): pieces = lax.all_to_all(pieces, 'ctx', 0, 0, tiled=True)  6.18 us
    ppermute x3, waiting for transfers between devices, swap(): return lax.ppermute(value, 'dp', [(i, i ^ flip) for i in range(groups)])  3.37 us
  transfers between devices with their start and end apart: 4, of which 4 were waited for; matrix products, arithmetic and copies ran while one was open for 1% of the time, Pallas kernels for 0%

profile of v3, /device:TPU:1, one launch (start us, length us, event | category | flops | bytes accessed | tf_op | source)
XLA Modules:
  0.0 37.9 jit_solution(14051479933338022460)
XLA Ops:
  0.0 0.0 copy-start.1
  0.0 0.0 copy-start
  0.0 11.0 %shard_map.235 = f32[16,7,256]{2,1,0:T(8,128)} custom-call(bf16[1,128,4096]{2,1,0:T(8,128)(2,1)} %refs_0_.1, bf16[1,128,4096]{2,1,0:T(8,128)(2,1)} %refs_1_.1, bf16[1,128,1024]{2,1,0:T(8,128)(2,1)} %refs_2_.1, bf16[1,128,1024]{2,1,0:T(8,128)(2,1)} %refs_3_.1, bf16[1,128,4096]{2,1,0:T(8,128)(2,1)} %refs_4_.1, bf16[1,128,4096]{2,1,0:T(8,128)(2,1)} %refs_5_.1, ...), custom_call_target="tpu_custom_call" | custom-call | flops 1140850688 | bytes 26738688 | tf_op jit(solution)/shard_map/pallas_call | solution.py:105
  11.0 7.6 %all-to-all-start = ((f32[16,7,256]{2,1,0:T(8,128)}), f32[16,7,256]{2,1,0:T(8,128)S(1)}, u32[]{:S(2)}, u32[]{:S(2)}) async-start(f32[16,7,256]{2,1,0:T(8,128)} %shard_map.235), calls=%async_computation | async-start | bytes 262144 | tf_op jit(solution)/shard_map/all_to_all | solution.py:148
  19.3 0.0 copy-done.1
  19.3 6.2 %all-to-all-done = f32[16,7,256]{2,1,0:T(8,128)S(1)} async-done(((f32[16,7,256]{2,1,0:T(8,128)}), f32[16,7,256]{2,1,0:T(8,128)S(1)}, u32[]{:S(2)}, u32[]{:S(2)}) %all-to-all-start) | async-done | bytes 114720 | tf_op jit(solution)/shard_map/all_to_all | solution.py:148
  25.5 0.1 select_reduce_fusion
  25.6 2.2 %collective-permute-start = (f32[7,256]{1,0:T(8,128)S(1)}, f32[7,256]{1,0:T(8,128)S(1)}, u32[]{:S(2)}, u32[]{:S(2)}) collective-permute-start(f32[7,256]{1,0:T(8,128)S(1)} %select_reduce_fusion), channel_id=1, source_target_pairs={{0,16},{16,0},{32,48},{48,32},{64,80},{80,64},{96,112},{112,96},{1... | collective-permute-start | bytes 21512 | tf_op jit(solution)/shard_map/ppermute | solution.py:137
  27.7 0.0 copy-done
  27.7 0.2 select_reduce_fusion.3
  27.9 0.6 %collective-permute-done = f32[7,256]{1,0:T(8,128)S(1)} collective-permute-done((f32[7,256]{1,0:T(8,128)S(1)}, f32[7,256]{1,0:T(8,128)S(1)}, u32[]{:S(2)}, u32[]{:S(2)}) %collective-permute-start) | collective-permute-done | bytes 7200 | tf_op jit(solution)/shard_map/ppermute | solution.py:137
  28.6 1.9 %collective-permute-start.1 = (f32[2,7,256]{2,0,1:T(2,128)S(1)}, f32[2,7,256]{2,0,1:T(2,128)S(1)}, u32[]{:S(2)}, u32[]{:S(2)}) collective-permute-start(f32[2,7,256]{2,0,1:T(2,128)S(1)} %pad_maximum_fusion.1), channel_id=1, source_target_pairs={{0,48},{16,32},{32,16},{48,0},{64,112},{80,96},{96,80},{112,64},{1... | collective-permute-start | bytes 43016 | tf_op jit(solution)/shard_map/ppermute | solution.py:137
  30.5 1.4 %collective-permute-done.1 = f32[2,7,256]{2,0,1:T(2,128)S(1)} collective-permute-done((f32[2,7,256]{2,0,1:T(2,128)S(1)}, f32[2,7,256]{2,0,1:T(2,128)S(1)}, u32[]{:S(2)}, u32[]{:S(2)}) %collective-permute-start.1) | collective-permute-done | bytes 14368 | tf_op jit(solution)/shard_map/ppermute | solution.py:137
  31.9 0.1 select_reduce_fusion.1
  32.0 3.9 %collective-permute-start.2 = (f32[7,256]{1,0:T(8,128)S(1)}, f32[7,256]{1,0:T(8,128)S(1)}, u32[]{:S(2)}, u32[]{:S(2)}) collective-permute-start(f32[7,256]{1,0:T(8,128)S(1)} %get-tuple-element.5), channel_id=1, source_target_pairs={{0,112},{16,96},{32,80},{48,64},{64,48},{80,32},{96,16},{112,0},{1... | collective-permute-start | bytes 21512 | tf_op jit(solution)/shard_map/ppermute | solution.py:137
  36.0 1.3 %collective-permute-done.2 = f32[7,256]{1,0:T(8,128)S(1)} collective-permute-done((f32[7,256]{1,0:T(8,128)S(1)}, f32[7,256]{1,0:T(8,128)S(1)}, u32[]{:S(2)}, u32[]{:S(2)}) %collective-permute-start.2) | collective-permute-done | bytes 7200 | tf_op jit(solution)/shard_map/ppermute | solution.py:137
  37.3 0.6 %copy.28 = f32[1,7,256]{2,0,1:T(1,128)} copy(f32[1,7,256]{2,1,0:T(8,128)S(1)} %add_bitcast_fusion) | data formatting | bytes 14336 | tf_op jit(solution)/shard_map/broadcast_in_dim | solution.py:142
  (7 shorter events, 0.0 us)
Async XLA Ops:
  0.0 19.3 %copy-start.1 = (s32[4]{0:T(128)S(1)}, s32[4]{0:T(128)}, u32[]{:S(2)}) copy-start(s32[4]{0:T(128)} %constant.16.clone) | copy-start | bytes 52
  0.0 27.7 %copy-start = (s32[8]{0:T(128)S(1)}, s32[8]{0:T(128)}, u32[]{:S(2)}) copy-start(s32[8]{0:T(128)} %param.48) | copy-start | bytes 100
  11.0 14.5 %all-to-all-start = ((f32[16,7,256]{2,1,0:T(8,128)}), f32[16,7,256]{2,1,0:T(8,128)S(1)}, u32[]{:S(2)}, u32[]{:S(2)}) async-start(f32[16,7,256]{2,1,0:T(8,128)} %shard_map.235), calls=%async_computation | async-start | bytes 262144 | tf_op jit(solution)/shard_map/all_to_all | solution.py:148
  25.6 3.0 %collective-permute-start = (f32[7,256]{1,0:T(8,128)S(1)}, f32[7,256]{1,0:T(8,128)S(1)}, u32[]{:S(2)}, u32[]{:S(2)}) collective-permute-start(f32[7,256]{1,0:T(8,128)S(1)} %select_reduce_fusion), channel_id=1, source_target_pairs={{0,16},{16,0},{32,48},{48,32},{64,80},{80,64},{96,112},{112,96},{1... | collective-permute-start | bytes 21512 | tf_op jit(solution)/shard_map/ppermute | solution.py:137
  28.6 3.4 %collective-permute-start.1 = (f32[2,7,256]{2,0,1:T(2,128)S(1)}, f32[2,7,256]{2,0,1:T(2,128)S(1)}, u32[]{:S(2)}, u32[]{:S(2)}) collective-permute-start(f32[2,7,256]{2,0,1:T(2,128)S(1)} %pad_maximum_fusion.1), channel_id=1, source_target_pairs={{0,48},{16,32},{32,16},{48,0},{64,112},{80,96},{96,80},{112,64},{1... | collective-permute-start | bytes 43016 | tf_op jit(solution)/shard_map/ppermute | solution.py:137
  32.0 5.3 %collective-permute-start.2 = (f32[7,256]{1,0:T(8,128)S(1)}, f32[7,256]{1,0:T(8,128)S(1)}, u32[]{:S(2)}, u32[]{:S(2)}) collective-permute-start(f32[7,256]{1,0:T(8,128)S(1)} %get-tuple-element.5), channel_id=1, source_target_pairs={{0,112},{16,96},{32,80},{48,64},{64,48},{80,32},{96,16},{112,0},{1... | collective-permute-start | bytes 21512 | tf_op jit(solution)/shard_map/ppermute | solution.py:137

commit v4 on v3

--- a/solution.py
+++ b/solution.py
@@ -38,8 +38,8 @@
     "seq_counts", "example_ids",
 )
 
-
 SLABS = 4
+PART = 7168
 
 
 def sketch_kernel(widths, *refs):
@@ -52,32 +52,42 @@
     square, act_sem, proj_sem = refs[1 + 4 * n :]
     rows = acts[ORDER[0]].shape[1]
 
-    copies = {
-        name: (
-            pltpu.make_async_copy(projs[name], proj_bufs[name], proj_sem.at[k]),
-            pltpu.make_async_copy(acts[name].at[0], act_bufs[name], act_sem.at[k]),
-        )
-        for k, name in enumerate(ORDER)
-    }
+    copies = {}
+    slot = 0
     for name in ORDER:
-        for copy in copies[name]:
-            copy.start()
+        copies[name] = []
+        for start in range(0, widths[name], PART):
+            part = pl.ds(start, min(PART, widths[name] - start))
+            pair = (
+                pltpu.make_async_copy(
+                    projs[name].at[:, part], proj_bufs[name].at[:, part], proj_sem.at[slot]
+                ),
+                pltpu.make_async_copy(
+                    acts[name].at[0, :, part], act_bufs[name].at[:, part], act_sem.at[slot]
+                ),
+            )
+            for copy in pair:
+                copy.start()
+            copies[name].append((start, part.size, pair))
+            slot += 1
 
     def project(name):
-        for copy in copies[name]:
-            copy.wait()
-        slab = widths[name] // SLABS
-        parts = [pl.ds(k * slab, slab) for k in range(SLABS)]
-        product = lax.dot_general(
-            jnp.concatenate([proj_bufs[name][:, part] for part in parts], axis=0),
-            jnp.concatenate([act_bufs[name][:, part] for part in parts], axis=0),
-            (((1,), (1,)), ((), ())),
-            preferred_element_type=jnp.float32,
-        )
-        blocks = [
-            product[k * RANK : (k + 1) * RANK, k * rows : (k + 1) * rows] for k in range(SLABS)
-        ]
-        return functools.reduce(jnp.add, blocks).astype(jnp.bfloat16)
+        total = None
+        for start, width, pair in copies[name]:
+            for copy in pair:
+                copy.wait()
+            slab = width // SLABS
+            slabs = [pl.ds(start + k * slab, slab) for k in range(SLABS)]
+            product = lax.dot_general(
+                jnp.concatenate([proj_bufs[name][:, at] for at in slabs], axis=0),
+                jnp.concatenate([act_bufs[name][:, at] for at in slabs], axis=0),
+                (((1,), (1,)), ((), ())),
+                preferred_element_type=jnp.float32,
+            )
+            for k in range(SLABS):
+                block = product[k * RANK : (k + 1) * RANK, k * rows : (k + 1) * rows]
+                total = block if total is None else total + block
+        return total.astype(jnp.bfloat16)
 
     for first, rest in GROUPS:
         inputs_proj = project(first)
@@ -102,6 +112,7 @@
     rows = values["attn_in"].shape[1]
     hbm = pl.BlockSpec(memory_space=pl.ANY)
     total = sum(widths.values())
+    parts = sum(-(-width // PART) for width in widths.values())
     return pl.pallas_call(
         functools.partial(sketch_kernel, widths),
         out_shape=jax.ShapeDtypeStruct((PIECES, len(MAPS), RANK * RANK // PIECES), jnp.float32),
@@ -111,8 +122,8 @@
             *[pltpu.VMEM((rows, widths[name]), jnp.bfloat16) for name in ORDER],
             *[pltpu.VMEM((RANK, widths[name]), jnp.bfloat16) for name in ORDER],
             pltpu.VMEM((len(MAPS) * RANK, RANK), jnp.float32),
-            pltpu.SemaphoreType.DMA((len(ORDER),)),
-            pltpu.SemaphoreType.DMA((len(ORDER),)),
+            pltpu.SemaphoreType.DMA((parts,)),
+            pltpu.SemaphoreType.DMA((parts,)),
         ],
         compiler_params=pltpu.CompilerParams(vmem_limit_bytes=60 * 1024 * 1024),
         cost_estimate=pl.CostEstimate(
@@ -131,14 +142,14 @@
     held = jnp.bitwise_xor(me, jnp.array([0, 1, 3, 2], jnp.int32))
     rows = jnp.sum(jnp.where(held[:, None] == slots[None, :], example_ids[None, :], 0), axis=1)
     keep = (rows == me)[:, None, None]
-    give = (rows == jnp.bitwise_xor(me, 7))[:, None, None]
+    give = (rows == jnp.bitwise_xor(me, 5))[:, None, None]
 
     def swap(value, flip):
         return lax.ppermute(value, "dp", [(i, i ^ flip) for i in range(groups)])
 
     two = jnp.stack([own, swap(own, 1)])
     four = jnp.concatenate([two, swap(two, 3)])
-    arrived = swap(jnp.sum(jnp.where(give, four, 0.0), axis=0), 7)
+    arrived = swap(jnp.sum(jnp.where(give, four, 0.0), axis=0), 5)
     return (jnp.sum(jnp.where(keep, four, 0.0), axis=0) + arrived)[None]
 
 

time: 38.1 us -> 37.7 us (0.990)
  no operation moved by 1% of the time
where the time goes in v4:
time: 37.7 us; the launch traced here: 37.5 us
  starting transfers between devices  15.5 us (41%)
  Pallas kernels  10.7 us (28%)
  waiting for transfers between devices  9.55 us (25%)
  between operations  0.71 us (2%)
  local copies, waits for them, and re-layouts  0.63 us (2%)
  other arithmetic  0.41 us (1%)
    pallas_call x1, Pallas kernels, sketches(): pl.pallas_call(functools.partial(sketch_kernel, widths), out_shape=jax.Sh...  10.7 us
    ppermute x3, starting transfers between devices, swap(): return lax.ppermute(value, 'dp', [(i, i ^ flip) for i in range(groups)])  7.89 us
    all_to_all x1, starting transfers between devices, shards(): pieces = lax.all_to_all(pieces, 'ctx', 0, 0, tiled=True)  7.59 us
    all_to_all x1, waiting for transfers between devices, shards(): pieces = lax.all_to_all(pieces, 'ctx', 0, 0, tiled=True)  6.19 us
    ppermute x3, waiting for transfers between devices, swap(): return lax.ppermute(value, 'dp', [(i, i ^ flip) for i in range(groups)])  3.37 us
  transfers between devices with their start and end apart: 4, of which 4 were waited for; matrix products, arithmetic and copies ran while one was open for 1% of the time, Pallas kernels for 0%

profile of v4, /device:TPU:1, one launch (start us, length us, event | category | flops | bytes accessed | tf_op | source)
XLA Modules:
  0.0 37.5 jit_solution(11922376003527335320)
XLA Ops:
  0.0 0.0 copy-start.1
  0.0 0.0 copy-start
  0.0 10.7 %shard_map.235 = f32[16,7,256]{2,1,0:T(8,128)} custom-call(bf16[1,128,4096]{2,1,0:T(8,128)(2,1)} %refs_0_.1, bf16[1,128,4096]{2,1,0:T(8,128)(2,1)} %refs_1_.1, bf16[1,128,1024]{2,1,0:T(8,128)(2,1)} %refs_2_.1, bf16[1,128,1024]{2,1,0:T(8,128)(2,1)} %refs_3_.1, bf16[1,128,4096]{2,1,0:T(8,128)(2,1)} %refs_4_.1, bf16[1,128,4096]{2,1,0:T(8,128)(2,1)} %refs_5_.1, ...), custom_call_target="tpu_custom_call" | custom-call | flops 1140850688 | bytes 26738688 | tf_op jit(solution)/shard_map/pallas_call | solution.py:116
  10.7 7.6 %all-to-all-start = ((f32[16,7,256]{2,1,0:T(8,128)}), f32[16,7,256]{2,1,0:T(8,128)S(1)}, u32[]{:S(2)}, u32[]{:S(2)}) async-start(f32[16,7,256]{2,1,0:T(8,128)} %shard_map.235), calls=%async_computation | async-start | bytes 262144 | tf_op jit(solution)/shard_map/all_to_all | solution.py:159
  19.0 0.0 copy-done.1
  19.0 6.2 %all-to-all-done = f32[16,7,256]{2,1,0:T(8,128)S(1)} async-done(((f32[16,7,256]{2,1,0:T(8,128)}), f32[16,7,256]{2,1,0:T(8,128)S(1)}, u32[]{:S(2)}, u32[]{:S(2)}) %all-to-all-start) | async-done | bytes 114720 | tf_op jit(solution)/shard_map/all_to_all | solution.py:159
  25.2 0.1 select_reduce_fusion
  25.3 2.2 %collective-permute-start = (f32[7,256]{1,0:T(8,128)S(1)}, f32[7,256]{1,0:T(8,128)S(1)}, u32[]{:S(2)}, u32[]{:S(2)}) collective-permute-start(f32[7,256]{1,0:T(8,128)S(1)} %select_reduce_fusion), channel_id=1, source_target_pairs={{0,16},{16,0},{32,48},{48,32},{64,80},{80,64},{96,112},{112,96},{1... | collective-permute-start | bytes 21512 | tf_op jit(solution)/shard_map/ppermute | solution.py:148
  27.5 0.0 copy-done
  27.5 0.2 select_reduce_fusion.3
  27.7 0.6 %collective-permute-done = f32[7,256]{1,0:T(8,128)S(1)} collective-permute-done((f32[7,256]{1,0:T(8,128)S(1)}, f32[7,256]{1,0:T(8,128)S(1)}, u32[]{:S(2)}, u32[]{:S(2)}) %collective-permute-start) | collective-permute-done | bytes 7200 | tf_op jit(solution)/shard_map/ppermute | solution.py:148
  28.3 1.9 %collective-permute-start.1 = (f32[2,7,256]{2,0,1:T(2,128)S(1)}, f32[2,7,256]{2,0,1:T(2,128)S(1)}, u32[]{:S(2)}, u32[]{:S(2)}) collective-permute-start(f32[2,7,256]{2,0,1:T(2,128)S(1)} %pad_maximum_fusion.1), channel_id=1, source_target_pairs={{0,48},{16,32},{32,16},{48,0},{64,112},{80,96},{96,80},{112,64},{1... | collective-permute-start | bytes 43016 | tf_op jit(solution)/shard_map/ppermute | solution.py:148
  30.3 1.4 %collective-permute-done.1 = f32[2,7,256]{2,0,1:T(2,128)S(1)} collective-permute-done((f32[2,7,256]{2,0,1:T(2,128)S(1)}, f32[2,7,256]{2,0,1:T(2,128)S(1)}, u32[]{:S(2)}, u32[]{:S(2)}) %collective-permute-start.1) | collective-permute-done | bytes 14368 | tf_op jit(solution)/shard_map/ppermute | solution.py:148
  31.7 0.1 select_reduce_fusion.1
  31.8 3.8 %collective-permute-start.2 = (f32[7,256]{1,0:T(8,128)S(1)}, f32[7,256]{1,0:T(8,128)S(1)}, u32[]{:S(2)}, u32[]{:S(2)}) collective-permute-start(f32[7,256]{1,0:T(8,128)S(1)} %get-tuple-element.5), channel_id=1, source_target_pairs={{0,80},{16,64},{32,112},{48,96},{64,16},{80,0},{96,48},{112,32},{1... | collective-permute-start | bytes 21512 | tf_op jit(solution)/shard_map/ppermute | solution.py:148
  35.6 1.3 %collective-permute-done.2 = f32[7,256]{1,0:T(8,128)S(1)} collective-permute-done((f32[7,256]{1,0:T(8,128)S(1)}, f32[7,256]{1,0:T(8,128)S(1)}, u32[]{:S(2)}, u32[]{:S(2)}) %collective-permute-start.2) | collective-permute-done | bytes 7200 | tf_op jit(solution)/shard_map/ppermute | solution.py:148
  36.9 0.6 %copy.28 = f32[1,7,256]{2,0,1:T(1,128)} copy(f32[1,7,256]{2,1,0:T(8,128)S(1)} %add_bitcast_fusion) | data formatting | bytes 14336 | tf_op jit(solution)/shard_map/broadcast_in_dim | solution.py:153
  (7 shorter events, 0.0 us)
Async XLA Ops:
  0.0 19.0 %copy-start.1 = (s32[4]{0:T(128)S(1)}, s32[4]{0:T(128)}, u32[]{:S(2)}) copy-start(s32[4]{0:T(128)} %constant.16.clone) | copy-start | bytes 52
  0.0 27.5 %copy-start = (s32[8]{0:T(128)S(1)}, s32[8]{0:T(128)}, u32[]{:S(2)}) copy-start(s32[8]{0:T(128)} %param.48) | copy-start | bytes 100
  10.7 14.5 %all-to-all-start = ((f32[16,7,256]{2,1,0:T(8,128)}), f32[16,7,256]{2,1,0:T(8,128)S(1)}, u32[]{:S(2)}, u32[]{:S(2)}) async-start(f32[16,7,256]{2,1,0:T(8,128)} %shard_map.235), calls=%async_computation | async-start | bytes 262144 | tf_op jit(solution)/shard_map/all_to_all | solution.py:159
  25.3 3.0 %collective-permute-start = (f32[7,256]{1,0:T(8,128)S(1)}, f32[7,256]{1,0:T(8,128)S(1)}, u32[]{:S(2)}, u32[]{:S(2)}) collective-permute-start(f32[7,256]{1,0:T(8,128)S(1)} %select_reduce_fusion), channel_id=1, source_target_pairs={{0,16},{16,0},{32,48},{48,32},{64,80},{80,64},{96,112},{112,96},{1... | collective-permute-start | bytes 21512 | tf_op jit(solution)/shard_map/ppermute | solution.py:148
  28.3 3.3 %collective-permute-start.1 = (f32[2,7,256]{2,0,1:T(2,128)S(1)}, f32[2,7,256]{2,0,1:T(2,128)S(1)}, u32[]{:S(2)}, u32[]{:S(2)}) collective-permute-start(f32[2,7,256]{2,0,1:T(2,128)S(1)} %pad_maximum_fusion.1), channel_id=1, source_target_pairs={{0,48},{16,32},{32,16},{48,0},{64,112},{80,96},{96,80},{112,64},{1... | collective-permute-start | bytes 43016 | tf_op jit(solution)/shard_map/ppermute | solution.py:148
  31.8 5.1 %collective-permute-start.2 = (f32[7,256]{1,0:T(8,128)S(1)}, f32[7,256]{1,0:T(8,128)S(1)}, u32[]{:S(2)}, u32[]{:S(2)}) collective-permute-start(f32[7,256]{1,0:T(8,128)S(1)} %get-tuple-element.5), channel_id=1, source_target_pairs={{0,80},{16,64},{32,112},{48,96},{64,16},{80,0},{96,48},{112,32},{1... | collective-permute-start | bytes 21512 | tf_op jit(solution)/shard_map/ppermute | solution.py:148

commit v5 on v4

--- a/solution.py
+++ b/solution.py
@@ -139,17 +139,17 @@
     groups = lax.axis_size("dp")
     me = lax.axis_index("dp")
     slots = jnp.arange(groups, dtype=jnp.int32)
-    held = jnp.bitwise_xor(me, jnp.array([0, 1, 3, 2], jnp.int32))
+    held = jnp.bitwise_xor(me, jnp.array([0, 1, 5, 4], jnp.int32))
     rows = jnp.sum(jnp.where(held[:, None] == slots[None, :], example_ids[None, :], 0), axis=1)
     keep = (rows == me)[:, None, None]
-    give = (rows == jnp.bitwise_xor(me, 5))[:, None, None]
+    give = (rows == jnp.bitwise_xor(me, 3))[:, None, None]
 
     def swap(value, flip):
         return lax.ppermute(value, "dp", [(i, i ^ flip) for i in range(groups)])
 
     two = jnp.stack([own, swap(own, 1)])
-    four = jnp.concatenate([two, swap(two, 3)])
-    arrived = swap(jnp.sum(jnp.where(give, four, 0.0), axis=0), 5)
+    four = jnp.concatenate([two, swap(two, 5)])
+    arrived = swap(jnp.sum(jnp.where(give, four, 0.0), axis=0), 3)
     return (jnp.sum(jnp.where(keep, four, 0.0), axis=0) + arrived)[None]
 
 

time: 37.7 us -> 37.7 us (level)
  starting transfers between devices: 15.5 us -> 15 us
  waiting for transfers between devices: 9.55 us -> 10 us
    ppermute x3, waiting for transfers between devices: 3.37 us -> 3.83 us  [swap(): return lax.ppermute(value, 'dp', [(i, i ^ flip) for i in range(groups)])]
    ppermute x3, starting transfers between devices: 7.89 us -> 7.42 us  [swap(): return lax.ppermute(value, 'dp', [(i, i ^ flip) for i in range(groups)])]
where the time goes in v5:
time: 37.7 us; the launch traced here: 37.5 us
  starting transfers between devices  15 us (40%)
  Pallas kernels  10.7 us (28%)
  waiting for transfers between devices  10 us (27%)
  between operations  0.71 us (2%)
  local copies, waits for them, and re-layouts  0.63 us (2%)
  other arithmetic  0.41 us (1%)
    pallas_call x1, Pallas kernels, sketches(): pl.pallas_call(functools.partial(sketch_kernel, widths), out_shape=jax.Sh...  10.7 us
    all_to_all x1, starting transfers between devices, shards(): pieces = lax.all_to_all(pieces, 'ctx', 0, 0, tiled=True)  7.59 us
    ppermute x3, starting transfers between devices, swap(): return lax.ppermute(value, 'dp', [(i, i ^ flip) for i in range(groups)])  7.42 us
    all_to_all x1, waiting for transfers between devices, shards(): pieces = lax.all_to_all(pieces, 'ctx', 0, 0, tiled=True)  6.19 us
    ppermute x3, waiting for transfers between devices, swap(): return lax.ppermute(value, 'dp', [(i, i ^ flip) for i in range(groups)])  3.83 us
  transfers between devices with their start and end apart: 4, of which 4 were waited for; matrix products, arithmetic and copies ran while one was open for 1% of the time, Pallas kernels for 0%

profile of v5, /device:TPU:1, one launch (start us, length us, event | category | flops | bytes accessed | tf_op | source)
XLA Modules:
  0.0 37.5 jit_solution(10846705494285252410)
XLA Ops:
  0.0 0.0 copy-start.1
  0.0 0.0 copy-start
  0.0 10.7 %shard_map.235 = f32[16,7,256]{2,1,0:T(8,128)} custom-call(bf16[1,128,4096]{2,1,0:T(8,128)(2,1)} %refs_0_.1, bf16[1,128,4096]{2,1,0:T(8,128)(2,1)} %refs_1_.1, bf16[1,128,1024]{2,1,0:T(8,128)(2,1)} %refs_2_.1, bf16[1,128,1024]{2,1,0:T(8,128)(2,1)} %refs_3_.1, bf16[1,128,4096]{2,1,0:T(8,128)(2,1)} %refs_4_.1, bf16[1,128,4096]{2,1,0:T(8,128)(2,1)} %refs_5_.1, ...), custom_call_target="tpu_custom_call" | custom-call | flops 1140850688 | bytes 26738688 | tf_op jit(solution)/shard_map/pallas_call | solution.py:116
  10.7 7.6 %all-to-all-start = ((f32[16,7,256]{2,1,0:T(8,128)}), f32[16,7,256]{2,1,0:T(8,128)S(1)}, u32[]{:S(2)}, u32[]{:S(2)}) async-start(f32[16,7,256]{2,1,0:T(8,128)} %shard_map.235), calls=%async_computation | async-start | bytes 262144 | tf_op jit(solution)/shard_map/all_to_all | solution.py:159
  19.0 0.0 copy-done.1
  19.0 6.2 %all-to-all-done = f32[16,7,256]{2,1,0:T(8,128)S(1)} async-done(((f32[16,7,256]{2,1,0:T(8,128)}), f32[16,7,256]{2,1,0:T(8,128)S(1)}, u32[]{:S(2)}, u32[]{:S(2)}) %all-to-all-start) | async-done | bytes 114720 | tf_op jit(solution)/shard_map/all_to_all | solution.py:159
  25.2 0.1 select_reduce_fusion
  25.3 2.2 %collective-permute-start = (f32[7,256]{1,0:T(8,128)S(1)}, f32[7,256]{1,0:T(8,128)S(1)}, u32[]{:S(2)}, u32[]{:S(2)}) collective-permute-start(f32[7,256]{1,0:T(8,128)S(1)} %select_reduce_fusion), channel_id=1, source_target_pairs={{0,16},{16,0},{32,48},{48,32},{64,80},{80,64},{96,112},{112,96},{1... | collective-permute-start | bytes 21512 | tf_op jit(solution)/shard_map/ppermute | solution.py:148
  27.5 0.0 copy-done
  27.5 0.2 select_reduce_fusion.3
  27.7 0.6 %collective-permute-done = f32[7,256]{1,0:T(8,128)S(1)} collective-permute-done((f32[7,256]{1,0:T(8,128)S(1)}, f32[7,256]{1,0:T(8,128)S(1)}, u32[]{:S(2)}, u32[]{:S(2)}) %collective-permute-start) | collective-permute-done | bytes 7200 | tf_op jit(solution)/shard_map/ppermute | solution.py:148
  28.3 3.9 %collective-permute-start.1 = (f32[2,7,256]{2,0,1:T(2,128)S(1)}, f32[2,7,256]{2,0,1:T(2,128)S(1)}, u32[]{:S(2)}, u32[]{:S(2)}) collective-permute-start(f32[2,7,256]{2,0,1:T(2,128)S(1)} %pad_maximum_fusion.1), channel_id=1, source_target_pairs={{0,80},{16,64},{32,112},{48,96},{64,16},{80,0},{96,48},{112,32},{1... | collective-permute-start | bytes 43016 | tf_op jit(solution)/shard_map/ppermute | solution.py:148
  32.2 1.4 %collective-permute-done.1 = f32[2,7,256]{2,0,1:T(2,128)S(1)} collective-permute-done((f32[2,7,256]{2,0,1:T(2,128)S(1)}, f32[2,7,256]{2,0,1:T(2,128)S(1)}, u32[]{:S(2)}, u32[]{:S(2)}) %collective-permute-start.1) | collective-permute-done | bytes 14368 | tf_op jit(solution)/shard_map/ppermute | solution.py:148
  33.6 0.1 select_reduce_fusion.1
  33.7 1.4 %collective-permute-start.2 = (f32[7,256]{1,0:T(8,128)S(1)}, f32[7,256]{1,0:T(8,128)S(1)}, u32[]{:S(2)}, u32[]{:S(2)}) collective-permute-start(f32[7,256]{1,0:T(8,128)S(1)} %get-tuple-element.5), channel_id=1, source_target_pairs={{0,48},{16,32},{32,16},{48,0},{64,112},{80,96},{96,80},{112,64},{1... | collective-permute-start | bytes 21512 | tf_op jit(solution)/shard_map/ppermute | solution.py:148
  35.1 1.8 %collective-permute-done.2 = f32[7,256]{1,0:T(8,128)S(1)} collective-permute-done((f32[7,256]{1,0:T(8,128)S(1)}, f32[7,256]{1,0:T(8,128)S(1)}, u32[]{:S(2)}, u32[]{:S(2)}) %collective-permute-start.2) | collective-permute-done | bytes 7200 | tf_op jit(solution)/shard_map/ppermute | solution.py:148
  36.9 0.6 %copy.28 = f32[1,7,256]{2,0,1:T(1,128)} copy(f32[1,7,256]{2,1,0:T(8,128)S(1)} %add_bitcast_fusion) | data formatting | bytes 14336 | tf_op jit(solution)/shard_map/broadcast_in_dim | solution.py:153
  (7 shorter events, 0.0 us)
Async XLA Ops:
  0.0 19.0 %copy-start.1 = (s32[4]{0:T(128)S(1)}, s32[4]{0:T(128)}, u32[]{:S(2)}) copy-start(s32[4]{0:T(128)} %constant.16.clone) | copy-start | bytes 52
  0.0 27.5 %copy-start = (s32[8]{0:T(128)S(1)}, s32[8]{0:T(128)}, u32[]{:S(2)}) copy-start(s32[8]{0:T(128)} %param.48) | copy-start | bytes 100
  10.7 14.5 %all-to-all-start = ((f32[16,7,256]{2,1,0:T(8,128)}), f32[16,7,256]{2,1,0:T(8,128)S(1)}, u32[]{:S(2)}, u32[]{:S(2)}) async-start(f32[16,7,256]{2,1,0:T(8,128)} %shard_map.235), calls=%async_computation | async-start | bytes 262144 | tf_op jit(solution)/shard_map/all_to_all | solution.py:159
  25.3 3.0 %collective-permute-start = (f32[7,256]{1,0:T(8,128)S(1)}, f32[7,256]{1,0:T(8,128)S(1)}, u32[]{:S(2)}, u32[]{:S(2)}) collective-permute-start(f32[7,256]{1,0:T(8,128)S(1)} %select_reduce_fusion), channel_id=1, source_target_pairs={{0,16},{16,0},{32,48},{48,32},{64,80},{80,64},{96,112},{112,96},{1... | collective-permute-start | bytes 21512 | tf_op jit(solution)/shard_map/ppermute | solution.py:148
  28.3 5.3 %collective-permute-start.1 = (f32[2,7,256]{2,0,1:T(2,128)S(1)}, f32[2,7,256]{2,0,1:T(2,128)S(1)}, u32[]{:S(2)}, u32[]{:S(2)}) collective-permute-start(f32[2,7,256]{2,0,1:T(2,128)S(1)} %pad_maximum_fusion.1), channel_id=1, source_target_pairs={{0,80},{16,64},{32,112},{48,96},{64,16},{80,0},{96,48},{112,32},{1... | collective-permute-start | bytes 43016 | tf_op jit(solution)/shard_map/ppermute | solution.py:148
  33.7 3.2 %collective-permute-start.2 = (f32[7,256]{1,0:T(8,128)S(1)}, f32[7,256]{1,0:T(8,128)S(1)}, u32[]{:S(2)}, u32[]{:S(2)}) collective-permute-start(f32[7,256]{1,0:T(8,128)S(1)} %get-tuple-element.5), channel_id=1, source_target_pairs={{0,48},{16,32},{32,16},{48,0},{64,112},{80,96},{96,80},{112,64},{1... | collective-permute-start | bytes 21512 | tf_op jit(solution)/shard_map/ppermute | solution.py:148
